TPU v7x, 32 devices: a whole 2x2x4 slice. The times are simulated.
32 devices in a mesh: module: 4 (over y, core), sample: 8 (over z, x).
Axes of the slice: x: 2, y: 2, z: 4, core: 2. Of those that a mesh axis runs over, the one named last changes fastest.
Arguments:
- queries: bfloat16 [16, 256, 4096], P('module', None, 'sample'), may hold values from -6 to 6
- inverse_hessian: bfloat16 [16, 4096, 4096], P('module', 'sample'), may hold values from -1 to 2.1, as said below
- train_grads: bfloat16 [16, 2560, 4096], P('module', 'sample'), may hold values from -0.09375 to 0.09375
Outputs:
- scores: float32 [2560, 256], P('sample')
Inputs may be any that keep to these rules, and one draw needn't show every extreme that they name: `inverse_hessian`: each module's matrix is symmetric.
All inputs are finite; a program needn't handle non-finite values.
Results may differ from a plain program's by a relative error of at most 0.0029.
Values may be sent and summed in bfloat16 or wider, within the bound.
A program may use at most 64 MiB of HBM per device.

v0:
```python
import jax
import jax.numpy as jnp
from jax import lax
from jax.sharding import PartitionSpec as P


def by_symmetry(query, slab, grads):
    share = lax.dot_general(
        slab,
        lax.all_gather(query, "sample", axis=1, tiled=True),
        (((1,), (1,)), ((), ())),
        preferred_element_type=jnp.float32,
    ).astype(jnp.bfloat16)
    return jnp.dot(
        grads,
        lax.all_gather(share, "sample", axis=0, tiled=True),
        preferred_element_type=jnp.float32,
    )


def on_device(queries, inverse_hessian, train_grads):
    total = jnp.zeros((train_grads.shape[1], queries.shape[1]), jnp.float32)
    for module_idx in range(queries.shape[0]):
        total = total + by_symmetry(
            queries[module_idx], inverse_hessian[module_idx], train_grads[module_idx]
        )
    return lax.psum(total, "module")


def solution(mesh):
    placed = (P("module", None, "sample"), P("module", "sample", None), P("module", "sample", None))
    return jax.shard_map(
        on_device, mesh=mesh, in_specs=placed, out_specs=P("sample", None), check_vma=False
    )
```

profile of v0, /device:TPU:0, one launch (start us, length us, event | category | flops | bytes accessed | tf_op | source)
XLA Modules:
  0.0 459.5 jit_solution(13458301935871993513)
XLA Ops:
  6.5 2.2 fusion.60
  8.7 0.0 all-gather.23.cloned.1.call-update
  8.7 0.0 all-gather.21.cloned.1.call-start
  8.8 0.7 all-gather.21.cloned.1.call-update
  9.5 0.0 all-gather.25.cloned.1.call-start
  9.5 0.7 all-gather.25.cloned.1.call-update
  10.2 0.0 all-gather.27.cloned.1.call-start
  10.3 0.5 all-gather.27.cloned.1.call-update
  10.8 0.0 all-gather.15.cloned.1.call-start
  10.8 52.4 %all-gather.23.cloned.1.call-done = bf16[1,256,4096]{2,1,0:T(8,128)(2,1)} async-done(((bf16[1,256,512]{2,1,0:T(8,128)(2,1)}), bf16[1,256,4096]{2,1,0:T(8,128)(2,1)}) %all-gather.23.cloned.1.call-update) | async-done | bytes 2097168 | tf_op jit(solution)/shard_map/all_gather | solution.py:10
  63.2 4.9 %fusion.33 = bf16[512,256]{1,0:T(8,128)(2,1)} fusion(bf16[1,256,4096]{2,1,0:T(8,128)(2,1)} %all-gather.23.cloned.1.call-done, bf16[4,512,4096]{2,1,0:T(8,128)(2,1)} %param.4), kind=kOutput, calls=%fused_computation.29 | convolution fusion | flops 1073872896 | bytes 6553600 | tf_op jit(solution)/shard_map/dot_general | solution.py:8
  68.1 0.0 all-gather.15.cloned.1.call-update
  68.1 0.0 all-gather.13.cloned.1.call-start
  68.2 46.4 %all-gather.21.cloned.1.call-done = bf16[1,256,4096]{2,1,0:T(8,128)(2,1)} async-done(((bf16[1,256,512]{2,1,0:T(8,128)(2,1)}), bf16[1,256,4096]{2,1,0:T(8,128)(2,1)}) %all-gather.21.cloned.1.call-update) | async-done | bytes 2097168 | tf_op jit(solution)/shard_map/all_gather | solution.py:10
  114.5 4.8 %fusion.28 = bf16[512,256]{1,0:T(8,128)(2,1)} fusion(bf16[1,256,4096]{2,1,0:T(8,128)(2,1)} %all-gather.21.cloned.1.call-done, bf16[4,512,4096]{2,1,0:T(8,128)(2,1)} %param.4), kind=kOutput, calls=%fused_computation.28 | convolution fusion | flops 1073872896 | bytes 6553600 | tf_op jit(solution)/shard_map/dot_general | solution.py:8
  119.4 0.0 all-gather.17.cloned.1.call-start
  119.5 46.4 %all-gather.25.cloned.1.call-done = bf16[1,256,4096]{2,1,0:T(8,128)(2,1)} async-done(((bf16[1,256,512]{2,1,0:T(8,128)(2,1)}), bf16[1,256,4096]{2,1,0:T(8,128)(2,1)}) %all-gather.25.cloned.1.call-update) | async-done | bytes 2097168 | tf_op jit(solution)/shard_map/all_gather | solution.py:10
  165.9 4.9 %fusion.38 = bf16[512,256]{1,0:T(8,128)(2,1)} fusion(bf16[1,256,4096]{2,1,0:T(8,128)(2,1)} %all-gather.25.cloned.1.call-done, bf16[4,512,4096]{2,1,0:T(8,128)(2,1)} %param.4), kind=kOutput, calls=%fused_computation.30 | convolution fusion | flops 1073872896 | bytes 6553600 | tf_op jit(solution)/shard_map/dot_general | solution.py:8
  170.8 0.0 all-gather.19.cloned.1.call-start
  170.8 46.2 %all-gather.27.cloned.1.call-done = bf16[1,256,4096]{2,1,0:T(8,128)(2,1)} async-done(((bf16[1,256,512]{2,1,0:T(8,128)(2,1)}), bf16[1,256,4096]{2,1,0:T(8,128)(2,1)}) %all-gather.27.cloned.1.call-update) | async-done | bytes 2097168 | tf_op jit(solution)/shard_map/all_gather | solution.py:10
  217.1 4.9 %fusion.43 = bf16[512,256]{1,0:T(8,128)(2,1)} fusion(bf16[1,256,4096]{2,1,0:T(8,128)(2,1)} %all-gather.27.cloned.1.call-done, bf16[4,512,4096]{2,1,0:T(8,128)(2,1)} %param.4), kind=kOutput, calls=%fused_computation.31 | convolution fusion | flops 1073872896 | bytes 6553600 | tf_op jit(solution)/shard_map/dot_general | solution.py:8
  222.0 0.0 all-reduce.2.cloned.1.call-start
  222.0 44.6 %all-gather.15.cloned.1.call-done = bf16[4096,256]{1,0:T(8,128)(2,1)} async-done(((bf16[512,256]{1,0:T(8,128)(2,1)}), bf16[4096,256]{1,0:T(8,128)(2,1)}) %all-gather.15.cloned.1.call-update) | async-done | bytes 2097168 | tf_op jit(solution)/shard_map/all_gather | solution.py:16
  266.6 3.2 fusion.16
  269.8 46.6 %all-gather.13.cloned.1.call-done = bf16[4096,256]{1,0:T(8,128)(2,1)} async-done(((bf16[512,256]{1,0:T(8,128)(2,1)}), bf16[4096,256]{1,0:T(8,128)(2,1)}) %all-gather.13.cloned.1.call-update) | async-done | bytes 2097168 | tf_op jit(solution)/shard_map/all_gather | solution.py:16
  316.4 3.2 fusion.48
  319.6 46.7 %all-gather.17.cloned.1.call-done = bf16[4096,256]{1,0:T(8,128)(2,1)} async-done(((bf16[512,256]{1,0:T(8,128)(2,1)}), bf16[4096,256]{1,0:T(8,128)(2,1)}) %all-gather.17.cloned.1.call-update) | async-done | bytes 2097168 | tf_op jit(solution)/shard_map/all_gather | solution.py:16
  366.3 3.2 fusion.51
  369.5 46.7 %all-gather.19.cloned.1.call-done = bf16[4096,256]{1,0:T(8,128)(2,1)} async-done(((bf16[512,256]{1,0:T(8,128)(2,1)}), bf16[4096,256]{1,0:T(8,128)(2,1)}) %all-gather.19.cloned.1.call-update) | async-done | bytes 2097168 | tf_op jit(solution)/shard_map/all_gather | solution.py:16
  416.2 3.9 fusion.57
  420.2 31.0 %all-reduce.2.cloned.1.call-done = f32[320,256]{1,0:T(8,128)} async-done(((f32[320,256]{1,0:T(8,128)}), f32[320,256]{1,0:T(8,128)}) %all-reduce.2.cloned.1.call-update) | async-done | bytes 327696 | tf_op jit(solution)/shard_map/psum | solution.py:27
  451.2 1.7 copy.5
  (5 shorter events, 0.1 us)
Async XLA Ops:
  6.5 56.7 %all-gather.23.cloned.1.call-start = ((), (), s32[]{:S(2)}) async-start(), calls=%async_computation.6 | async-start | bytes 2359296 | tf_op jit(solution)/shard_map/all_gather | solution.py:10
  8.7 105.8 %all-gather.21.cloned.1.call-start = ((), (), s32[]{:S(2)}) async-start(), calls=%async_computation.5 | async-start | bytes 2359296 | tf_op jit(solution)/shard_map/all_gather | solution.py:10
  9.5 156.4 %all-gather.25.cloned.1.call-start = ((), (), s32[]{:S(2)}) async-start(), calls=%async_computation.7 | async-start | bytes 2359296 | tf_op jit(solution)/shard_map/all_gather | solution.py:10
  10.2 206.9 %all-gather.27.cloned.1.call-start = ((), (), s32[]{:S(2)}) async-start(), calls=%async_computation.8 | async-start | bytes 2359296 | tf_op jit(solution)/shard_map/all_gather | solution.py:10
  10.8 255.8 %all-gather.15.cloned.1.call-start = ((), (), s32[]{:S(2)}) async-start(), calls=%async_computation.1 | async-start | bytes 2359296 | tf_op jit(solution)/shard_map/all_gather | solution.py:16
  68.1 248.2 %all-gather.13.cloned.1.call-start = ((), (), s32[]{:S(2)}) async-start(), calls=%async_computation | async-start | bytes 2359296 | tf_op jit(solution)/shard_map/all_gather | solution.py:16
  119.4 246.9 %all-gather.17.cloned.1.call-start = ((), (), s32[]{:S(2)}) async-start(), calls=%async_computation.2 | async-start | bytes 2359296 | tf_op jit(solution)/shard_map/all_gather | solution.py:16
  170.8 245.4 %all-gather.19.cloned.1.call-start = ((), (), s32[]{:S(2)}) async-start(), calls=%async_computation.3 | async-start | bytes 2359296 | tf_op jit(solution)/shard_map/all_gather | solution.py:16
  222.0 229.2 %all-reduce.2.cloned.1.call-start = ((), (), s32[]{:S(2)}) async-start(), calls=%async_computation.4 | async-start | bytes 655360 | tf_op jit(solution)/shard_map/psum | solution.py:27
Sparse Core Ops, SparseCore 0:
  9.4 53.7 all-gather.22
  65.2 49.2 all-gather.20
  116.6 49.2 all-gather.24
  167.8 49.2 all-gather.26
  219.1 47.4 all-gather.14
  268.5 47.7 all-gather.12
  318.5 47.7 all-gather.16
  368.4 47.7 all-gather.18
  420.3 30.8 all-reduce.1
where the time goes:
time: 460 us; the launch traced here: 459 us
  waiting for transfers between devices  409 us (89%)
  matrix products  33.1 us (7%)
  between operations  13.2 us (3%)
    all_gather x4, waiting for transfers between devices, by_symmetry(): lax.all_gather(query, 'sample', axis=1, tiled=True)  191 us
    all_gather x4, waiting for transfers between devices, by_symmetry(): lax.all_gather(share, 'sample', axis=0, tiled=True)  185 us
    psum x1, waiting for transfers between devices, on_device(): return lax.psum(total, 'module')  31 us
    dot_general x4, matrix products, by_symmetry(): lax.dot_general(slab, lax.all_gather(query, 'sample', axis=1, tiled=True)...  19.4 us
    dot_general x4, matrix products, by_symmetry(): jnp.dot(grads, lax.all_gather(share, 'sample', axis=0, tiled=True), prefe...  13.6 us
  transfers between devices with their start and end apart: 9, of which 9 were waited for; matrix products, arithmetic and copies ran while one was open for 6% of the time, Pallas kernels for 0%

commit v1 on v0

v1 whole, which is shorter than its diff:
```python
import functools

import jax
import jax.numpy as jnp
from jax import lax
from jax.experimental import pallas as pl
from jax.experimental.pallas import tpu as pltpu
from jax.sharding import PartitionSpec as P

PAIR = 2
ROWS = 16
LANES = 128
NT = (((1,), (1,)), ((), ()))


def by_symmetry(query, slab, grads):
    share = lax.dot_general(
        slab,
        lax.all_gather(query, "sample", axis=1, tiled=True),
        NT,
        preferred_element_type=jnp.float32,
    ).astype(jnp.bfloat16)
    return jnp.dot(
        grads,
        lax.all_gather(share, "sample", axis=0, tiled=True),
        preferred_element_type=jnp.float32,
    )


def by_gather(queries, inverse_hessian, train_grads):
    total = jnp.zeros((train_grads.shape[1], queries.shape[1]), jnp.float32)
    for module_idx in range(queries.shape[0]):
        total = total + by_symmetry(
            queries[module_idx], inverse_hessian[module_idx], train_grads[module_idx]
        )
    return lax.psum(total, "module")


def pieces_of(rows):
    cross = rows * 3 // 16 // ROWS * ROWS
    half = (rows - cross + 1) // 2
    half = (half + ROWS - 1) // ROWS * ROWS
    return ((0, half, False), (half, rows - cross - half, False), (rows - cross, cross, True))


def ladder(
    n, q_hbm, h_hbm, g_hbm, out_ref, blocks, h, g, acc, recv, zsend, xsend, q_sem, h_sem, g_sem
):
    modules, rows, wide = q_hbm.shape
    items = 2 * modules
    levels = n // PAIR
    pieces = pieces_of(rows)
    me = lax.axis_index("sample")
    z, x = me // PAIR, me % PAIR
    other = 1 - x

    q_loads = [
        pltpu.make_async_copy(q_hbm.at[m], blocks.at[m, me], q_sem.at[m]) for m in range(modules)
    ]
    for load in q_loads:
        load.start()
    for m in range(modules):
        pltpu.make_async_copy(h_hbm.at[m], h.at[m], h_sem.at[m]).start()
    for m in range(modules):
        pltpu.make_async_copy(g_hbm.at[m], g.at[m], g_sem.at[m]).start()

    barrier = pltpu.get_barrier_semaphore()
    greeted = (
        lax.rem(z + 1, levels) * PAIR + x,
        lax.rem(z + levels - 1, levels) * PAIR + x,
        z * PAIR + other,
    )
    for device in greeted:
        pl.semaphore_signal(
            barrier, inc=1, device_id={"sample": device}, device_id_type=pl.DeviceIdType.MESH
        )
    pl.semaphore_wait(barrier, len(greeted))

    out_ref[...] = jnp.zeros_like(out_ref)
    for load in q_loads:
        load.wait()

    def copy(i, p, level, column, sem, device):
        first, count, _ = pieces[p]
        slot = level * PAIR + column
        ref = blocks.at[i, slot, pl.ds(first, count)]
        return pltpu.make_async_remote_copy(
            src_ref=ref,
            dst_ref=ref,
            send_sem=sem,
            recv_sem=recv.at[i, p, slot],
            device_id={"sample": device},
            device_id_type=pl.DeviceIdType.MESH,
        )

    def up(i, p, level, column, act):
        @pl.when(z < levels - 1)
        def _():
            act(copy(i, p, level, column, zsend.at[i, p, column, level], me + PAIR))

    def down(i, p, level, column, act):
        @pl.when(z > 0)
        def _():
            act(copy(i, p, level, column, zsend.at[i, p, column, level + 1], me - PAIR))

    def across(i, p, level, act):
        act(copy(i, p, level, x, xsend.at[i, p, level], z * PAIR + other))

    def arrived(i, p, level, column):
        copy(i, p, level, column, xsend.at[i, p, level], me).wait_recv()

    def own(i, act):
        for p in range(len(pieces)):
            up(i, p, z, x, act)
            down(i, p, z, x, act)
            across(i, p, z, act)

    def relay(i, act, wait):
        for p, (_, _, crosses) in enumerate(pieces):
            if crosses:
                if wait:
                    arrived(i, p, z, other)
                up(i, p, z, other, act)
                down(i, p, z, other, act)
        for d in range(1, levels):
            for p, (_, _, crosses) in enumerate(pieces):

                @pl.when(z >= d)
                def _():
                    for column in (x, other) if crosses else (x,):
                        if wait:
                            arrived(i, p, z - d, column)
                        up(i, p, z - d, column, act)
                    if not crosses:
                        across(i, p, z - d, act)

                @pl.when(z + d < levels)
                def _():
                    for column in (x, other) if crosses else (x,):
                        if wait:
                            arrived(i, p, z + d, column)
                        down(i, p, z + d, column, act)
                    if not crosses:
                        across(i, p, z + d, act)

    def crossed(i):
        for p, (_, _, crosses) in enumerate(pieces):
            if not crosses:
                for level in range(levels):
                    arrived(i, p, level, other)

    def columns(s):
        return pl.ds(pl.multiple_of(s * wide, LANES), wide)

    def precondition(m):
        pltpu.make_async_copy(h_hbm.at[m], h.at[m], h_sem.at[m]).wait()
        acc[...] = jnp.zeros_like(acc)

        @pl.loop(0, n)
        def _(s):
            acc[...] += lax.dot_general(
                blocks[m, s], h[m, :, columns(s)], NT, preferred_element_type=jnp.float32
            )

        blocks[modules + m, me] = acc[...].astype(blocks.dtype)

    def score(m):
        pltpu.make_async_copy(g_hbm.at[m], g.at[m], g_sem.at[m]).wait()

        @pl.loop(0, n)
        def _(s):
            out_ref[...] += lax.dot_general(
                g[m, :, columns(s)], blocks[modules + m, s], NT, preferred_element_type=jnp.float32
            )

    own(0, lambda c: c.start())

    @pl.loop(0, items + 1)
    def _(t):
        @pl.when(t + 1 < items)
        def _():
            own(t + 1, lambda c: c.start())

        @pl.when(t < items)
        def _():
            relay(t, lambda c: c.start(), True)

        @pl.when(t > 0)
        def _():
            crossed(t - 1)

        @pl.when((t > 0) & (t <= modules))
        def _():
            precondition(t - 1)

        @pl.when(t > modules)
        def _():
            score(t - 1 - modules)

    @pl.loop(0, items)
    def _(t):
        own(t, lambda c: c.wait_send())
        relay(t, lambda c: c.wait_send(), False)


def by_ladder(n, queries, inverse_hessian, train_grads):
    modules, rows, wide = queries.shape
    samples, depth = train_grads.shape[1:]
    levels = n // PAIR
    items = 2 * modules
    count = len(pieces_of(rows))
    kind = queries.dtype
    total = pl.pallas_call(
        functools.partial(ladder, n),
        out_shape=jax.ShapeDtypeStruct((samples, rows), jnp.float32),
        in_specs=[pl.BlockSpec(memory_space=pl.ANY)] * 3,
        out_specs=pl.BlockSpec(memory_space=pltpu.VMEM),
        scratch_shapes=[
            pltpu.VMEM((items, n, rows, wide), kind),
            pltpu.VMEM((modules, wide, depth), kind),
            pltpu.VMEM((modules, samples, depth), kind),
            pltpu.VMEM((rows, wide), jnp.float32),
            pltpu.SemaphoreType.DMA((items, count, n)),
            pltpu.SemaphoreType.DMA((items, count, PAIR, levels + 1)),
            pltpu.SemaphoreType.DMA((items, count, levels)),
            pltpu.SemaphoreType.DMA((modules,)),
            pltpu.SemaphoreType.DMA((modules,)),
            pltpu.SemaphoreType.DMA((modules,)),
        ],
        compiler_params=pltpu.CompilerParams(
            collective_id=0, has_side_effects=True, vmem_limit_bytes=56 * 2**20
        ),
    )(queries, inverse_hessian, train_grads)
    return lax.psum(total, "module")


def solution(mesh):
    n = mesh.shape["sample"]

    def on_device(queries, inverse_hessian, train_grads):
        _, rows, wide = queries.shape
        if wide % LANES or rows % ROWS or n % PAIR or n <= 2 * PAIR:
            return by_gather(queries, inverse_hessian, train_grads)
        return by_ladder(n, queries, inverse_hessian, train_grads)

    placed = (P("module", None, "sample"), P("module", "sample", None), P("module", "sample", None))
    return jax.shard_map(
        on_device, mesh=mesh, in_specs=placed, out_specs=P("sample", None), check_vma=False
    )
```

time: 460 us -> 230 us (0.50)
  waiting for transfers between devices: 409 us -> 31.8 us
  Pallas kernels: 0 us -> 183 us
  matrix products: 33.1 us -> 0 us
    all_gather x8 -> x0, waiting for transfers between devices: 376 us -> none  [the longest x4 191 us: by_symmetry(): lax.all_gather(query, 'sample', axis=1, tiled=True)]
    pallas_call x0 -> x1, Pallas kernels: none -> 183 us  [by_ladder(): pl.pallas_call(functools.partial(ladder, n), out_shape=jax.ShapeDtypeStru...]
    dot_general x8 -> x0, matrix products: 33.1 us -> none  [the longest x4 19.4 us: by_symmetry(): lax.dot_general(slab, lax.all_gather(query, 'sample', axis=1, tiled=True)...]
  transfers between devices with their start and end apart: 9 -> 1, of which waited for: 9 -> 1; matrix products, arithmetic and copies ran while one was open for 6% -> 0% of each run, Pallas kernels for 0% -> 0%
where the time goes in v1:
time: 230 us; the launch traced here: 229 us
  Pallas kernels  183 us (80%)
  waiting for transfers between devices  31.8 us (14%)
  between operations  13.4 us (6%)
    pallas_call x1, Pallas kernels, by_ladder(): pl.pallas_call(functools.partial(ladder, n), out_shape=jax.ShapeDtypeStru...  183 us
    psum x1, waiting for transfers between devices, by_ladder(): return lax.psum(total, 'module')  31.8 us
  transfers between devices with their start and end apart: 1, of which 1 were waited for; matrix products, arithmetic and copies ran while one was open for 0% of the time, Pallas kernels for 0%

profile of v1, /device:TPU:0, one launch (start us, length us, event | category | flops | bytes accessed | tf_op | source)
XLA Modules:
  0.0 229.5 jit_solution(4077756707521747828)
XLA Ops:
  6.5 0.0 all-reduce.2.cloned.1.call-start
  6.5 182.6 %shard_map.37 = f32[320,256]{1,0:T(8,128)} custom-call(bf16[4,256,512]{2,1,0:T(8,128)(2,1)} %q_hbm.1, bf16[4,512,4096]{2,1,0:T(8,128)(2,1)} %h_hbm.1, bf16[4,320,4096]{2,1,0:T(8,128)(2,1)} %g_hbm.1), custom_call_target="tpu_custom_call" | custom-call | tf_op jit(solution)/shard_map/pallas_call | solution.py:213
  189.1 0.0 all-reduce.2.cloned.1.call-update
  189.2 31.8 %all-reduce.2.cloned.1.call-done = f32[320,256]{1,0:T(8,128)} async-done(((f32[320,256]{1,0:T(8,128)}), f32[320,256]{1,0:T(8,128)}) %all-reduce.2.cloned.1.call-update) | async-done | bytes 327696 | tf_op jit(solution)/shard_map/psum | solution.py:234
  220.9 1.7 copy.6
Async XLA Ops:
  6.5 214.4 %all-reduce.2.cloned.1.call-start = ((), (), s32[]{:S(2)}) async-start(), calls=%async_computation | async-start | bytes 655360 | tf_op jit(solution)/shard_map/psum | solution.py:234
Sparse Core Ops, SparseCore 0:
  189.3 31.5 all-reduce.1

commit v2 on v1

--- a/solution.py
+++ b/solution.py
@@ -10,6 +10,7 @@
 PAIR = 2
 ROWS = 16
 LANES = 128
+AHEAD = 2
 NT = (((1,), (1,)), ((), ()))
 
 
@@ -44,7 +45,7 @@
 
 
 def ladder(
-    n, q_hbm, h_hbm, g_hbm, out_ref, blocks, h, g, acc, recv, zsend, xsend, q_sem, h_sem, g_sem
+    n, q_hbm, h_hbm, g_hbm, out_ref, blocks, h, g, acc, halves, recv, zsend, xsend, q_sem, h_sem, g_sem, sum_send, sum_recv
 ):
     modules, rows, wide = q_hbm.shape
     items = 2 * modules
@@ -70,11 +71,19 @@
         lax.rem(z + levels - 1, levels) * PAIR + x,
         z * PAIR + other,
     )
+    group = lax.axis_index("module")
+    chip, core = group // PAIR, group % PAIR
+    twin = chip * PAIR + 1 - core
+    beyond = (1 - chip) * PAIR + core
     for device in greeted:
         pl.semaphore_signal(
             barrier, inc=1, device_id={"sample": device}, device_id_type=pl.DeviceIdType.MESH
         )
-    pl.semaphore_wait(barrier, len(greeted))
+    for device in (twin, beyond):
+        pl.semaphore_signal(
+            barrier, inc=1, device_id={"module": device}, device_id_type=pl.DeviceIdType.MESH
+        )
+    pl.semaphore_wait(barrier, len(greeted) + 2)
 
     out_ref[...] = jnp.zeros_like(out_ref)
     for load in q_loads:
@@ -173,13 +182,15 @@
                 g[m, :, columns(s)], blocks[modules + m, s], NT, preferred_element_type=jnp.float32
             )
 
-    own(0, lambda c: c.start())
+    ahead = min(AHEAD, modules - 2)
+    for i in range(ahead):
+        own(i, lambda c: c.start())
 
     @pl.loop(0, items + 1)
     def _(t):
-        @pl.when(t + 1 < items)
-        def _():
-            own(t + 1, lambda c: c.start())
+        @pl.when(t + ahead < items)
+        def _():
+            own(t + ahead, lambda c: c.start())
 
         @pl.when(t < items)
         def _():
@@ -196,6 +207,29 @@
         @pl.when(t > modules)
         def _():
             score(t - 1 - modules)
+
+    half = out_ref.shape[0] // PAIR
+    kept = pl.ds(pl.multiple_of(core * half, 8), half)
+    given = pl.ds(pl.multiple_of((1 - core) * half, 8), half)
+
+    def exchange(step, rows, device):
+        move = pltpu.make_async_remote_copy(
+            src_ref=out_ref.at[rows],
+            dst_ref=halves.at[step],
+            send_sem=sum_send.at[step],
+            recv_sem=sum_recv.at[step],
+            device_id={"module": device},
+            device_id_type=pl.DeviceIdType.MESH,
+        )
+        move.start()
+        move.wait()
+
+    exchange(0, given, twin)
+    out_ref[kept] += halves[0]
+    exchange(1, kept, beyond)
+    out_ref[kept] += halves[1]
+    exchange(2, kept, twin)
+    out_ref[given] = halves[2]
 
     @pl.loop(0, items)
     def _(t):
@@ -210,7 +244,7 @@
     items = 2 * modules
     count = len(pieces_of(rows))
     kind = queries.dtype
-    total = pl.pallas_call(
+    return pl.pallas_call(
         functools.partial(ladder, n),
         out_shape=jax.ShapeDtypeStruct((samples, rows), jnp.float32),
         in_specs=[pl.BlockSpec(memory_space=pl.ANY)] * 3,
@@ -220,26 +254,30 @@
             pltpu.VMEM((modules, wide, depth), kind),
             pltpu.VMEM((modules, samples, depth), kind),
             pltpu.VMEM((rows, wide), jnp.float32),
+            pltpu.VMEM((3, samples // PAIR, rows), jnp.float32),
             pltpu.SemaphoreType.DMA((items, count, n)),
             pltpu.SemaphoreType.DMA((items, count, PAIR, levels + 1)),
             pltpu.SemaphoreType.DMA((items, count, levels)),
             pltpu.SemaphoreType.DMA((modules,)),
             pltpu.SemaphoreType.DMA((modules,)),
             pltpu.SemaphoreType.DMA((modules,)),
+            pltpu.SemaphoreType.DMA((3,)),
+            pltpu.SemaphoreType.DMA((3,)),
         ],
         compiler_params=pltpu.CompilerParams(
             collective_id=0, has_side_effects=True, vmem_limit_bytes=56 * 2**20
         ),
     )(queries, inverse_hessian, train_grads)
-    return lax.psum(total, "module")
 
 
 def solution(mesh):
-    n = mesh.shape["sample"]
+    n, groups = mesh.shape["sample"], mesh.shape["module"]
 
     def on_device(queries, inverse_hessian, train_grads):
-        _, rows, wide = queries.shape
-        if wide % LANES or rows % ROWS or n % PAIR or n <= 2 * PAIR:
+        modules, rows, wide = queries.shape
+        aligned = wide % LANES == 0 and rows % ROWS == 0 and train_grads.shape[1] % ROWS == 0
+        ladders = n % PAIR == 0 and n > 2 * PAIR and groups == PAIR * PAIR
+        if not (aligned and ladders and modules > 2):
             return by_gather(queries, inverse_hessian, train_grads)
         return by_ladder(n, queries, inverse_hessian, train_grads)
 

time: 230 us -> 194 us (0.84)
  waiting for transfers between devices: 31.8 us -> 0 us
  between operations: 13.4 us -> 0.01 us
  Pallas kernels: 183 us -> 192 us
    psum x1 -> x0, waiting for transfers between devices: 31.8 us -> none  [by_ladder(): return lax.psum(total, 'module')]
    pallas_call x1, Pallas kernels: 183 us -> 192 us  [by_ladder(): pl.pallas_call(functools.partial(ladder, n), out_shape=jax.ShapeDtypeStru...]
  transfers between devices with their start and end apart: 1 -> 0, of which waited for: 1 -> 0; matrix products, arithmetic and copies ran while one was open for 0% -> 0% of each run, Pallas kernels for 0% -> 0%
where the time goes in v2:
time: 194 us
  Pallas kernels  192 us (99%)
    pallas_call x1, Pallas kernels, by_ladder(): pl.pallas_call(functools.partial(ladder, n), out_shape=jax.ShapeDtypeStru...  192 us

profile of v2, /device:TPU:0, one launch (start us, length us, event | category | flops | bytes accessed | tf_op | source)
XLA Modules:
  0.0 193.6 jit_solution(15242298251218378528)
XLA Ops:
  0.0 191.9 %shard_map.37 = f32[320,256]{1,0:T(8,128)} custom-call(bf16[4,256,512]{2,1,0:T(8,128)(2,1)} %q_hbm.1, bf16[4,512,4096]{2,1,0:T(8,128)(2,1)} %h_hbm.1, bf16[4,320,4096]{2,1,0:T(8,128)(2,1)} %g_hbm.1), custom_call_target="tpu_custom_call" | custom-call | tf_op jit(solution)/shard_map/pallas_call | solution.py:247
  191.9 1.7 copy.5
